TPU v7x, 128 devices: a whole 4x4x4 slice. The times are simulated.
128 devices in a mesh: replica: 4 (over x_hi, core), fsdp: 32 (over y, z, x_lo).
Axes of the slice: x: 4 (x_hi: 2, x_lo: 2; x = x_hi * 2 + x_lo), y: 4, z: 4, core: 2. Of those that a mesh axis runs over, the one named last changes fastest.
Arguments:
- tokens: bfloat16 [98304, 8192], P(('replica', 'fsdp')), may hold values from -24 to 24
- sign_bits: int32 [8192], replicated, may hold values from 0 to 1
- base_weight: bfloat16 [8192, 1024], P('fsdp'), may hold values from -0.0625 to 0.0625
- learned_column_scale: float32 [1024], replicated, may hold values from 0.5 to 2
- adapter_in: bfloat16 [4, 8192, 256], P('replica', 'fsdp'), may hold values from -0.0625 to 0.0625
- adapter_up_weight: bfloat16 [4, 256, 1024], P('replica'), may hold values from -0.375 to 0.375
- out_cotangent: bfloat16 [98304, 1024], P(('replica', 'fsdp')), may hold values from -6 to 6
- local_left: float32 [4, 4, 8192, 256], P('replica', None, 'fsdp'), may hold values from -6 to 6
- local_right: float32 [4, 4, 256, 1024], P('replica', None, 'fsdp'), may hold values from -6 to 6
- global_left: float32 [4, 8192, 256], P(None, 'fsdp'), may hold values from -6 to 6
- global_right: float32 [4, 256, 1024], P(None, 'fsdp'), may hold values from -6 to 6
- moment_left: float32 [4, 8192, 256], P(None, 'fsdp'), may hold values from -4 to 4
- moment_right: float32 [4, 256, 1024], P(None, 'fsdp'), may hold values from -4 to 4
- pending_left: float32 [4, 8192, 256], P(None, 'fsdp'), may hold values from -6 to 6
- pending_right: float32 [4, 256, 1024], P(None, 'fsdp'), may hold values from -6 to 6
Outputs:
- values: bfloat16 [98304, 1024], P(('replica', 'fsdp'))
- grad_in: float32 [4, 8192, 256], P('replica', 'fsdp')
- grad_out: float32 [4, 256, 1024], P('replica', 'fsdp')
- grad_scale: float32 [4, 1024], P('replica')
- next_global_left: float32 [4, 8192, 256], P(None, 'fsdp')
- next_global_right: float32 [4, 256, 1024], P(None, 'fsdp')
- next_moment_left: float32 [4, 8192, 256], P(None, 'fsdp')
- next_moment_right: float32 [4, 256, 1024], P(None, 'fsdp')
- next_pending_left: float32 [4, 8192, 256], P(None, 'fsdp')
- next_pending_right: float32 [4, 256, 1024], P(None, 'fsdp')
All inputs are finite; a program needn't handle non-finite values.
Results may differ from a plain program's by a relative error of at most 0.012.
Values may be sent and summed in bfloat16 or wider, within the bound.
A program may use at most 192 MiB of HBM per device.

v0:
```python
import math

import jax
import jax.numpy as jnp
from jax import lax
from jax.sharding import PartitionSpec as P

ADAPTER_SCALE = 2.0
MOMENTUM = 0.9
OUTER_RATE = 0.7


def hadamard_matrix(order_size):
    indices = jnp.arange(order_size, dtype=jnp.int32)
    parity = jnp.zeros((order_size, order_size), jnp.int32)
    for bit_pos in range(order_size.bit_length() - 1):
        upper = jnp.bitwise_and(jnp.right_shift(indices, bit_pos), 1)
        parity = parity + upper[:, None] * upper[None, :]
    return (1 - 2 * (parity % 2)).astype(jnp.bfloat16)


def rotate(tokens, sign_bits):
    features = tokens.shape[1]
    block_list = features // 128
    sign_flipped = tokens * (1 - 2 * sign_bits).astype(jnp.bfloat16)
    first_section = jnp.einsum(
        "lvr,rq->lvq",
        sign_flipped.reshape(-1, block_list, 128),
        hadamard_matrix(128),
        preferred_element_type=jnp.float32,
    ).astype(jnp.bfloat16)
    section_two = jnp.einsum(
        "tab,ac->tcb",
        first_section,
        hadamard_matrix(block_list),
        preferred_element_type=jnp.float32,
    ) * (1.0 / math.sqrt(features))
    return section_two.astype(jnp.bfloat16).reshape(-1, features)


def fragment_step(
    local_left,
    local_right,
    global_left,
    global_right,
    moment_left,
    moment_right,
    pending_left,
    pending_right,
    copies,
):
    delta_sum = (
        lax.psum((global_left - local_left[0]).astype(jnp.bfloat16), "replica").astype(jnp.float32),
        lax.psum((global_right - local_right[0]).astype(jnp.bfloat16), "replica").astype(
            jnp.float32
        ),
    )
    next_moment_left = MOMENTUM * moment_left + pending_left
    next_moment_right = MOMENTUM * moment_right + pending_right
    next_global_left = global_left - OUTER_RATE * (pending_left + MOMENTUM * next_moment_left)
    next_global_right = global_right - OUTER_RATE * (pending_right + MOMENTUM * next_moment_right)
    return (
        next_global_left,
        next_global_right,
        next_moment_left,
        next_moment_right,
        delta_sum[0] / copies,
        delta_sum[1] / copies,
    )


def per_device(
    tokens,
    sign_bits,
    base_weight,
    learned_column_scale,
    adapter_in,
    adapter_up_weight,
    out_cotangent,
    local_left,
    local_right,
    global_left,
    global_right,
    moment_left,
    moment_right,
    pending_left,
    pending_right,
):
    groups = lax.axis_size("fsdp")
    copies = lax.axis_size("replica")
    rows_here = tokens.shape[0]
    shrink_factor = 1.0 / math.sqrt(rows_here * groups)
    rotated = rotate(tokens, sign_bits)
    inner_left = adapter_in[0]
    inner_right = adapter_up_weight[0]
    frozen_output = jnp.dot(
        rotated,
        lax.all_gather(base_weight, "fsdp", axis=0, tiled=True),
        preferred_element_type=jnp.float32,
    )
    low_sum = jnp.dot(
        tokens,
        lax.all_gather(inner_left, "fsdp", axis=0, tiled=True),
        preferred_element_type=jnp.float32,
    )
    low_rank_product = low_sum.astype(jnp.bfloat16)
    rotated_mixture = frozen_output * learned_column_scale + ADAPTER_SCALE * jnp.dot(
        low_rank_product, inner_right, preferred_element_type=jnp.float32
    )
    values = rotated_mixture.astype(jnp.bfloat16)
    output_gradient = out_cotangent.astype(jnp.float32)
    grad_scale = lax.psum(jnp.sum(output_gradient * frozen_output, axis=0) * shrink_factor, "fsdp")
    out_term = lax.dot_general(
        low_rank_product,
        out_cotangent,
        (((0,), (0,)), ((), ())),
        preferred_element_type=jnp.float32,
    ) * (ADAPTER_SCALE * shrink_factor)
    grad_out = lax.psum_scatter(out_term, "fsdp", scatter_dimension=0, tiled=True)
    backward_rank_term = (
        lax.dot_general(
            out_cotangent, inner_right, (((1,), (1,)), ((), ())), preferred_element_type=jnp.float32
        )
        * ADAPTER_SCALE
    ).astype(jnp.bfloat16)
    grad_in = lax.psum_scatter(
        lax.dot_general(
            tokens, backward_rank_term, (((0,), (0,)), ((), ())), preferred_element_type=jnp.float32
        )
        * shrink_factor,
        "fsdp",
        scatter_dimension=0,
        tiled=True,
    )
    updated = fragment_step(
        local_left,
        local_right,
        global_left,
        global_right,
        moment_left,
        moment_right,
        pending_left,
        pending_right,
        copies,
    )
    return (
        values,
        grad_in[None],
        grad_out[None],
        grad_scale[None],
        updated[0],
        updated[1],
        updated[2],
        updated[3],
        updated[4],
        updated[5],
    )


def solution(mesh):
    return jax.shard_map(
        per_device,
        mesh=mesh,
        in_specs=(
            P(("replica", "fsdp"), None),
            P(),
            P("fsdp", None),
            P(),
            P("replica", "fsdp", None),
            P("replica", None, None),
            P(("replica", "fsdp"), None),
            P("replica", None, "fsdp", None),
            P("replica", None, "fsdp", None),
            P(None, "fsdp", None),
            P(None, "fsdp", None),
            P(None, "fsdp", None),
            P(None, "fsdp", None),
            P(None, "fsdp", None),
            P(None, "fsdp", None),
        ),
        out_specs=(
            P(("replica", "fsdp"), None),
            P("replica", "fsdp", None),
            P("replica", "fsdp", None),
            P("replica", None),
            P(None, "fsdp", None),
            P(None, "fsdp", None),
            P(None, "fsdp", None),
            P(None, "fsdp", None),
            P(None, "fsdp", None),
            P(None, "fsdp", None),
        ),
        check_vma=False,
    )
```

profile of v0, /device:TPU:0, one launch (start us, length us, event | category | flops | bytes accessed | tf_op | source)
XLA Modules:
  0.0 919.1 jit_solution(13378636285759833778)
XLA Ops:
  8.0 0.0 copy-start
  8.0 0.0 all-reduce.3.cloned.1.call-start
  8.1 4.0 multiply_subtract_fusion
  12.0 1.8 multiply_subtract_fusion.1
  13.9 0.0 all-reduce.3.cloned.1.call-update
  13.9 0.0 all-gather.6.cloned.1.call-start
  14.0 0.5 all-gather.6.cloned.1.call-update
  14.5 0.0 copy-start.2
  14.5 0.0 reduce-scatter.3.cloned.1.call-start
  14.5 0.0 copy-done
  14.6 11.4 %fusion.5 = f32[8192,256]{0,1:T(8,128)} fusion(bf16[768,8192]{1,0:T(8,128)(2,1)} %param.15, bf16[768,1024]{1,0:T(8,128)(2,1)} %param.21, bf16[1,256,1024]{2,1,0:T(8,128)(2,1)S(1)} %copy-done), kind=kOutput, calls=%fused_computation.8 | convolution fusion | flops 3626369024 | bytes 23068672 | tf_op jit(solution)/shard_map/dot_general | solution.py:127
  26.0 0.0 reduce-scatter.3.cloned.1.call-update
  26.0 0.0 all-gather.4.cloned.1.call-start
  26.0 0.5 all-gather.4.cloned.1.call-update
  26.6 0.0 reduce-scatter.5.cloned.1.call-start
  26.6 6.1 multiply_bitcast_fusion
  32.8 6.6 copy.26
  39.4 13.0 %multiply_convert_fusion = bf16[64,768,128]{2,0,1:T(8,128)(2,1)} fusion(bf16[768,64,128]{2,1,0:T(8,128)(2,1)} %bitcast.49, s32[128]{0:T(128)S(1)} %get-tuple-element.30, s32[128]{0:T(128)S(1)} %get-tuple-element.31, s32[128]{0:T(128)S(1)} %get-tuple-element.32, s32[128]{0:T(128)S(1)} %get-tuple-element.33, s32[128]{0:T(128)S(1)} %get-tuple-element.34, ...), kind=kOutput, calls=%fused_computation | convolution fusion | flops 2435338240 | bytes 25170944 | tf_op jit(solution)/shard_map/tab,ac->tcb/dot_general | solution.py:32
  52.4 10.8 %all-reduce.3.cloned.1.call-done = (bf16[4,256,256]{2,1,0:T(8,128)(2,1)}, bf16[4,8,1024]{2,1,0:T(8,128)(2,1)}) async-done(((bf16[4,256,256]{2,1,0:T(8,128)(2,1)}, bf16[4,8,1024]{2,1,0:T(8,128)(2,1)}), (bf16[4,256,256]{2,1,0:T(8,128)(2,1)}, bf16[4,8,1024]{2,1,0:T(8,128)(2,1)})) %all-reduce.3.cloned.1.call-update) | async-done | bytes 589840 | tf_op jit(solution)/shard_map/psum | solution.py:53
  63.2 1.6 convert_multiply_fusion.1
  64.8 2.1 convert_multiply_fusion
  66.9 120.6 %all-gather.6.cloned.1.call-done = bf16[1,8192,256]{2,1,0:T(8,128)(2,1)} async-done(((bf16[1,256,256]{2,1,0:T(8,128)(2,1)}), bf16[1,8192,256]{2,1,0:T(8,128)(2,1)}) %all-gather.6.cloned.1.call-update) | async-done | bytes 4194320 | tf_op jit(solution)/shard_map/all_gather | solution.py:103
  187.5 9.2 fusion.13
  196.7 1.6 convolution_multiply_fusion.1
  198.3 0.0 reduce-scatter.5.cloned.1.call-update
  198.3 187.3 %reduce-scatter.3.cloned.1.call-done = f32[256,256]{0,1:T(8,128)} async-done(((f32[8192,256]{0,1:T(8,128)}), f32[256,256]{0,1:T(8,128)}) %reduce-scatter.3.cloned.1.call-update) | async-done | bytes 262160 | tf_op jit(solution)/shard_map/reduce_scatter | solution.py:126
  385.6 1.8 copy.25
  387.4 361.5 %all-gather.4.cloned.1.call-done = bf16[8192,1024]{1,0:T(8,128)(2,1)} async-done(((bf16[256,1024]{1,0:T(8,128)(2,1)}), bf16[8192,1024]{1,0:T(8,128)(2,1)}) %all-gather.4.cloned.1.call-update) | async-done | bytes 16777232 | tf_op jit(solution)/shard_map/all_gather | solution.py:98
  748.9 21.4 %multiply_reduce_fusion = (f32[1024]{0:T(1024)S(1)}, f32[768,1024]{1,0:T(8,128)}) fusion(bf16[768,1024]{1,0:T(8,128)(2,1)S(1)} %copy-done.1, bf16[8192,1024]{1,0:T(8,128)(2,1)} %all-gather.4.cloned.1.call-done, bf16[96,8,64,128]{3,2,1,0:T(8,128)(2,1)} %bitcast.50), kind=kOutput, calls=%fused_computation.12 | convolution fusion | flops 12887260160 | bytes 34082816 | tf_op jit(solution)/shard_map/dot_general | solution.py:96
  770.4 78.8 %psum.21 = f32[1,1024]{1,0:T(1,128)} all-reduce(f32[1,1024]{1,0:T(1,128)S(1)} %bitcast.52), channel_id=1, replica_groups=mesh['replica'=4,'fsdp'=32] {'fsdp'}, use_global_device_ids=true, to_apply=%region_3.4 | all-reduce | flops 1024 | bytes 8192 | tf_op jit(solution)/shard_map/psum | solution.py:112
  849.2 3.6 add_convert_fusion
  852.8 58.7 %reduce-scatter.5.cloned.1.call-done = f32[8,1024]{1,0:T(8,128)} async-done(((f32[256,1024]{1,0:T(8,128)}), f32[8,1024]{1,0:T(8,128)}) %reduce-scatter.5.cloned.1.call-update) | async-done | bytes 32784 | tf_op jit(solution)/shard_map/reduce_scatter | solution.py:119
  (14 shorter events, 0.1 us)
Async XLA Ops:
  8.0 6.5 copy-start
  8.0 55.1 %all-reduce.3.cloned.1.call-start = ((), (), s32[]{:S(2)}) async-start(), calls=%async_computation.6 | async-start | bytes 1179648 | tf_op jit(solution)/shard_map/psum | solution.py:53
  13.9 173.6 %all-gather.6.cloned.1.call-start = ((), (), s32[]{:S(2)}) async-start(), calls=%async_computation.5 | async-start | bytes 4325376 | tf_op jit(solution)/shard_map/all_gather | solution.py:103
  14.5 12.1 %copy-start.2 = (s32[8192]{0:T(1024)S(1)}, s32[8192]{0:T(1024)}, u32[]{:S(2)}) copy-start(s32[8192]{0:T(1024)} %param.16) | copy-start | bytes 98308
  14.5 371.1 %reduce-scatter.3.cloned.1.call-start = ((), (), s32[]{:S(2)}) async-start(), calls=%async_computation.3 | async-start | bytes 8650752 | tf_op jit(solution)/shard_map/reduce_scatter | solution.py:126
  26.0 723.0 %all-gather.4.cloned.1.call-start = ((), (), s32[]{:S(2)}) async-start(), calls=%async_computation.2 | async-start | bytes 17301504 | tf_op jit(solution)/shard_map/all_gather | solution.py:98
  26.6 884.9 %reduce-scatter.5.cloned.1.call-start = ((), (), s32[]{:S(2)}) async-start(), calls=%async_computation.4 | async-start | bytes 1081344 | tf_op jit(solution)/shard_map/reduce_scatter | solution.py:119
  63.2 133.6 %copy-start.1 = (bf16[768,1024]{1,0:T(8,128)(2,1)S(1)}, bf16[768,1024]{1,0:T(8,128)(2,1)}, u32[]{:S(2)}) copy-start(bf16[768,1024]{1,0:T(8,128)(2,1)} %param.21) | copy-start | bytes 4718596
  748.9 100.2 %copy-start.3 = (f32[1024]{0:T(1024)S(1)}, f32[1024]{0:T(1024)}, u32[]{:S(2)}) copy-start(f32[1024]{0:T(1024)} %param.18) | copy-start | bytes 12292
Sparse Core Ops, SparseCore 0:
  14.0 49.1 all-reduce.2
Sparse Core Ops, SparseCore 1:
  16.0 171.5 all-gather.5
  189.8 195.8 reduce-scatter.2
  387.2 361.7 all-gather.3
  751.9 159.5 reduce-scatter.4
where the time goes:
time: 919 us
  waiting for transfers between devices  740 us (81%)
  blocking collectives  78.8 us (9%)
  matrix products  60.2 us (7%)
  between operations  15.8 us (2%)
  other arithmetic  15.7 us (2%)
    all_gather x1, waiting for transfers between devices, per_device(): lax.all_gather(base_weight, 'fsdp', axis=0, tiled=True)  362 us
    reduce_scatter x1, waiting for transfers between devices, per_device(): lax.psum_scatter(lax.dot_general(tokens, backward_rank_term, (((0,), (0,)...  187 us
    all_gather x1, waiting for transfers between devices, per_device(): lax.all_gather(inner_left, 'fsdp', axis=0, tiled=True)  121 us
    psum x1, blocking collectives, per_device(): lax.psum(jnp.sum(output_gradient * frozen_output, axis=0) * shrink_factor...  78.8 us
    reduce_scatter x1, waiting for transfers between devices, per_device(): lax.psum_scatter(out_term, 'fsdp', scatter_dimension=0, tiled=True)  58.7 us
    dot_general x1, matrix products, per_device(): jnp.dot(rotated, lax.all_gather(base_weight, 'fsdp', axis=0, tiled=True),...  21.4 us
  transfers between devices with their start and end apart: 5, of which 5 were waited for; matrix products, arithmetic and copies ran while one was open for 9% of the time, Pallas kernels for 0%

commit v1 on v0

v1 whole, which is shorter than its diff:
```python
import math

import jax
import jax.numpy as jnp
import numpy as np
from jax import lax
from jax.experimental import pallas as pl
from jax.experimental.pallas import tpu as pltpu
from jax.sharding import PartitionSpec as P

MESH = pl.DeviceIdType.MESH
BF = jnp.bfloat16
F32 = jnp.float32
ADAPTER_SCALE = 2.0
MOMENTUM = 0.9
OUTER_RATE = 0.7
ROWS = 768
NSEM = 160


def hadamard(n):
    i = np.arange(n)
    both = i[:, None] & i[None, :]
    parity = np.zeros((n, n), np.int64)
    for b in range(n.bit_length()):
        parity += (both >> b) & 1
    return (1 - 2 * (parity % 2)).astype(np.float32)


def nt(a, b):
    return lax.dot_general(a, b, (((1,), (1,)), ((), ())), preferred_element_type=F32)


def nn(a, b):
    return jnp.dot(a, b, preferred_element_type=F32)


def body(
    tokens, sign, weight, scale, a_in, up, cot, ll, lr, gl, gr, ml, mr, pend_l, pend_r, had,
    o_val, o_gin, o_gout, o_gs, o_gl, o_gr, o_ml, o_mr, o_pl, o_pr,
    wg, ag, tok, st, sl, g, r1, r2, r3, r4, r5, cotv, upv, acc, low, bt, val, signv, scalev, hadv, wsh,
    go, go_o, go_i, go_x, go_f, gs, gs_o, fl, fr, dl, dr, dl1, dr1, dl2, dr2, gin, gout,
    send, recv, loc, st_sem, sl_sem,
):
    r, f = lax.axis_index("replica"), lax.axis_index("fsdp")
    xh, c = r // 2, r % 2
    y, z, xl = f // 8, (f // 2) % 4, f % 2
    c1, xl1 = 1 - c, 1 - xl
    shrink = 1.0 / math.sqrt(ROWS * 32)

    def dev(dx=0, dy=0, dz=0, dc=0):
        x = (2 * xh + xl + dx + 4) % 4
        return ((x // 2) * 2 + (c + dc) % 2, ((y + dy + 4) % 4) * 8 + ((z + dz + 4) % 4) * 2 + x % 2)

    def xpair():
        return (r, y * 8 + z * 2 + xl1)

    def mod4(v):
        return (v + 4) % 4

    nloc = [0]

    def local(src, dst):
        cp = pltpu.make_async_copy(src, dst, loc.at[nloc[0]])
        nloc[0] += 1
        cp.start()
        return cp

    nrem = [0]
    sent = []

    def push(src, dst, where):
        k = nrem[0]
        nrem[0] += 1
        cp = pltpu.make_async_remote_copy(
            src_ref=src, dst_ref=dst, send_sem=send.at[k], recv_sem=recv.at[k],
            device_id=where, device_id_type=MESH,
        )
        cp.start()
        sent.append(cp)
        return cp

    def row_copy(k):
        rows = pl.ds(pl.multiple_of(k * 48, 48), 48)
        return pltpu.make_async_copy(tokens.at[rows], st.at[k % 2], st_sem.at[k % 2])

    def col_copy(k):
        cols = pl.ds(pl.multiple_of(k * 512, 512), 512)
        return pltpu.make_async_copy(tokens.at[:, cols], sl.at[k % 2], sl_sem.at[k % 2])

    ld_w = local(weight.at[:, pl.ds(pl.multiple_of(c * 512, 512), 512)], wsh)
    ld_h = local(had, hadv)
    ld_a = local(a_in, ag.at[y, z, xl])
    ld_up = local(up, upv)
    ld_cot = local(cot, cotv)
    ld_tok = [local(tokens.at[:, pl.ds(k * 1024, 1024)], tok.at[:, pl.ds(k * 1024, 1024)]) for k in range(8)]
    row_copy(0).start()
    col_copy(0).start()
    ld_s = local(sign, signv)
    ld_sc = local(scale, scalev)
    ld_f = [local(s, fl.at[k]) for k, s in enumerate((ll, gl, ml, pend_l))]
    ld_f += [local(s, fr.at[k]) for k, s in enumerate((lr, gr, mr, pend_r))]

    barrier = pltpu.get_barrier_semaphore()
    peers = [dev(dx=1), dev(dx=-1), dev(dx=2), dev(dy=1), dev(dy=-1), dev(dy=2), dev(dz=1), dev(dz=-1), dev(dz=2), dev(dc=1)]
    for p in peers:
        pl.semaphore_signal(barrier, inc=1, device_id=p, device_id_type=MESH)

    ld_w.wait()
    ld_h.wait()
    w1 = (nn(hadv[...], wsh[...]) * (1.0 / math.sqrt(8192))).astype(BF)
    wg[c, 0, xl, y, z] = w1[:128]
    wg[c, 1, xl, z, y] = w1[128:]
    pl.semaphore_wait(barrier, len(peers))

    pos = [(y, z), (z, y)]

    def out_dev(q, d):
        return dev(dy=d) if q == 0 else dev(dz=d)

    def in_dev(q, d):
        return dev(dz=d) if q == 0 else dev(dy=d)

    w_in, w_out, w_x, w_sib = [{}, {}], [{}, {}], [{}, {}], [{}, {}]

    def wgrp(q, xv, d, ch=None):
        return wg.at[c if ch is None else ch, q, xv, mod4(pos[q][0] + d)]

    def w_in1(q):
        o, i = pos[q]
        ref = wg.at[c, q, xl, o, i]
        for d in (1, -1):
            w_in[q][d] = push(ref, ref, in_dev(q, d))

    def w_in2(q):
        o, i = pos[q]
        for d, h in ((1, 0), (-1, 64)):
            w_in[q][d].wait_recv()
            ref = wg.at[c, q, xl, o, mod4(i - d), pl.ds(h, 64)]
            w_in[q][2 * d] = push(ref, ref, in_dev(q, d))

    def w_share(q, d):
        ref = wgrp(q, xl, d)
        w_x[q][d] = push(ref, ref, dev(dx=-1 if q == 0 else 1))
        w_sib[q][0, d] = push(ref, ref, dev(dc=1))

    def w_out1(q):
        for d in (1, -1):
            w_in[q][2 * d].wait_recv()
        ref = wgrp(q, xl, 0)
        for d in (1, -1):
            w_out[q][d] = push(ref, ref, out_dev(q, d))
        w_share(q, 0)

    def w_out2(q):
        for d, h in ((1, 0), (-1, 2)):
            w_out[q][d].wait_recv()
            ref = wg.at[c, q, xl, mod4(pos[q][0] - d), pl.ds(h, 2)]
            w_out[q][2 * d] = push(ref, ref, out_dev(q, d))
        for d in (1, -1):
            w_share(q, d)

    def w_out3(q):
        for d in (1, -1):
            w_out[q][2 * d].wait_recv()
        w_share(q, 2)

    def w_x1(q, d):
        w_x[q][d].wait_recv()
        ref = wgrp(q, xl1, d)
        w_sib[q][1, d] = push(ref, ref, dev(dc=1))

    a_x, a_i, a_o = {}, [{}, {}], [{}, {}]

    def apiece(q, i, xs=slice(None)):
        return ag.at[y, i, xs, 0] if q == 0 else ag.at[i, z, xs, 1]

    def agrp(q, o, i=slice(None)):
        return ag.at[o, i, :, 0] if q == 0 else ag.at[i, o, :, 1]

    def a_x1():
        ld_a.wait()
        a_x[0] = push(ag.at[y, z, xl], ag.at[y, z, xl], xpair())

    def a_in1(q):
        if q == 0:
            a_x[0].wait_recv()
        ref = apiece(q, pos[q][1])
        for d in (1, -1):
            a_i[q][d] = push(ref, ref, in_dev(q, d))

    def a_in2(q):
        for d, h in ((1, 0), (-1, 1)):
            a_i[q][d].wait_recv()
            ref = apiece(q, mod4(pos[q][1] - d), h)
            a_i[q][2 * d] = push(ref, ref, in_dev(q, d))

    def a_out1(q):
        for d in (1, -1):
            a_i[q][2 * d].wait_recv()
        ref = agrp(q, pos[q][0])
        for d in (1, -1):
            a_o[q][d] = push(ref, ref, out_dev(q, d))

    def a_out2(q):
        for d, h in ((1, 0), (-1, 2)):
            a_o[q][d].wait_recv()
            ref = agrp(q, mod4(pos[q][0] - d), pl.ds(h, 2))
            a_o[q][2 * d] = push(ref, ref, out_dev(q, d))

    def a_out3(q):
        for d in (1, -1):
            a_o[q][2 * d].wait_recv()

    rs = [{}, {}]

    def gidx(q, o, i, xv):
        return (o, i, xv, 0) if q == 0 else (i, o, xv, 1)

    def ggrp(q, o, i=slice(None)):
        return g.at[o, i, :, 0] if q == 0 else g.at[i, o, :, 1]

    def add_to(q, o, i, xv, *terms):
        at = gidx(q, o, i, xv)
        total = g[at].astype(F32)
        for t in terms:
            total = total + t.astype(F32)
        g[at] = total.astype(BF)

    def rs_1(q):
        o = mod4(pos[q][0] + 2)
        for k, (d, h) in enumerate(((1, 0), (-1, 2))):
            rs[q][1, d] = push(ggrp(q, o, pl.ds(h, 2)), r1.at[q, k], out_dev(q, d))

    def rs_2(q):
        for k, (d, h) in enumerate(((1, 0), (-1, 2))):
            rs[q][1, d].wait_recv()
            o = mod4(pos[q][0] + d)

            def one(j, carry, k=k, h=h, o=o):
                add_to(q, o, h + j // 2, j % 2, r1[q, k, j // 2, j % 2])
                return carry

            lax.fori_loop(0, 4, one, 0)
            rs[q][2, d] = push(ggrp(q, o), r2.at[q, k], out_dev(q, d))

    def rs_3(q):
        for d in (1, -1):
            rs[q][2, d].wait_recv()

        def one(j, carry):
            add_to(q, pos[q][0], j // 2, j % 2, r2[q, 0, j // 2, j % 2], r2[q, 1, j // 2, j % 2])
            return carry

        lax.fori_loop(0, 8, one, 0)

    def gpiece(q, i, xs=slice(None)):
        return g.at[y, i, xs, 0] if q == 0 else g.at[i, z, xs, 1]

    def rs_4(q):
        i = mod4(pos[q][1] + 2)
        for k, d in enumerate((1, -1)):
            rs[q][4, d] = push(gpiece(q, i, k), r3.at[q, k], in_dev(q, d))

    def rs_5(q):
        for k, d in enumerate((1, -1)):
            rs[q][4, d].wait_recv()
            i = mod4(pos[q][1] + d)
            add_to(q, pos[q][0], i, k, r3[q, k])
            rs[q][5, d] = push(gpiece(q, i), r4.at[q, k], in_dev(q, d))

    def rs_6(q):
        for d in (1, -1):
            rs[q][5, d].wait_recv()
        for k in range(2):
            add_to(q, pos[q][0], pos[q][1], k, r4[q, 0, k], r4[q, 1, k])
        rs[q][6] = push(gpiece(q, pos[q][1], xl1), r5.at[q], xpair())

    def rs_7(q):
        rs[q][6].wait_recv()
        total = g[gidx(q, pos[q][0], pos[q][1], xl)].astype(F32) + r5[q].astype(F32)
        gin[:, q * 128 : (q + 1) * 128] = (total * shrink).T

    def back():
        ld_up.wait()
        ld_cot.wait()
        for k in range(3):
            bt[:, k * 256 : (k + 1) * 256] = (nt(upv[...], cotv[k * 256 : (k + 1) * 256, :]) * ADAPTER_SCALE).astype(BF)

    def grad_in(ks):
        for k in ks:
            ld_tok[k].wait()

        def one(j, carry):
            cols = pl.ds(pl.multiple_of(j * 256, 256), 256)
            part = nn(bt[...], tok[:, cols]).astype(BF)
            g[j // 8, (j // 2) % 4, j % 2, 0] = part[:128]
            g[j // 8, (j // 2) % 4, j % 2, 1] = part[128:]
            return carry

        lax.fori_loop(ks[0] * 4, ks[-1] * 4 + 4, one, 0)

    def rotate(lo, hi):
        def chunk(k, carry):
            row_copy(k).wait()

            @pl.when(k + 1 < 16)
            def _():
                row_copy(k + 1).start()

            lax.fori_loop(0, 6, lambda j, n: rotate_rows(k, j, n), 0)
            return carry

        lax.fori_loop(lo, hi, chunk, 0)

    def rotate_rows(chunk, k, carry):
        at = pl.multiple_of((k // 2) * 16, 16)
        rows = pl.ds(pl.multiple_of(chunk * 48 + at, 16), 16)
        q = k % 2
        parts = []
        for j in range(32):
            cols = pl.ds(pl.multiple_of(j * 256 + q * 128, 128), 128)
            parts.append(st[chunk % 2, pl.ds(at, 16), cols].astype(F32) * signv[:, cols])
        for b in range(5):
            step = 1 << b
            for j in range(32):
                if not j & step:
                    u, v = parts[j], parts[j + step]
                    parts[j], parts[j + step] = u + v, u - v
        for j in range(32):
            jy, jz, jx = j // 8, (j // 2) % 4, j % 2
            t = q * 32 + jx * 16 + (1 - q) * (jy * 4 + jz) + q * (jz * 4 + jy)
            tok[rows, pl.ds(pl.multiple_of(t * 128, 128), 128)] = parts[j].astype(BF)
        return carry

    def frozen(q, xv, d, ch, first=False):
        o = mod4(pos[q][0] + d)
        at = pl.multiple_of(((q * 2 + xv) * 4 + o) * 512, 512)
        part = nn(tok[:, pl.ds(at, 512)], wg[ch, q, xv, o].reshape(512, 512))
        if first:
            acc[ch] = part
        else:
            acc[ch] += part

    def low_rank():
        def one(k, carry):
            col_copy(k).wait()

            @pl.when(k + 1 < 16)
            def _():
                col_copy(k + 1).start()

            part = nn(sl[k % 2], ag[k // 4, k % 4].reshape(512, 256))
            low[...] = jnp.where(k == 0, part, low[...] + part)
            return carry

        lax.fori_loop(0, 16, one, 0)

    fx = {}

    def frag_1():
        for cp in ld_f:
            cp.wait()
        for buf, d in ((fl, dl), (fr, dr)):
            n = buf.shape[1]
            for h in range(2):
                rows = slice(h * n // 2, (h + 1) * n // 2)
                lv, gv, mv, pv = (buf[k, rows] for k in range(4))
                nm = MOMENTUM * mv + pv
                buf[2, rows] = nm
                buf[0, rows] = gv - OUTER_RATE * (pv + MOMENTUM * nm)
                d[h] = (gv - lv).astype(BF)
        fx["l"] = push(dl.at[c1], dl1, dev(dc=1))
        fx["r"] = push(dr.at[c1], dr1, dev(dc=1))
        return [local(fl.at[0], o_gl), local(fr.at[0], o_gr), local(fl.at[2], o_ml), local(fr.at[2], o_mr)]

    def frag_2():
        for k, d, d1, d2 in (("l", dl, dl1, dl2), ("r", dr, dr1, dr2)):
            fx[k].wait_recv()
            d1[...] = (d1[...].astype(F32) + d[c].astype(F32)).astype(BF)
            fx[k + "x"] = push(d1, d2, dev(dx=2))

    def frag_3():
        for k, d1, d2, buf in (("l", dl1, dl2, fl), ("r", dr1, dr2, fr)):
            fx[k + "x"].wait_recv()
            n = buf.shape[1] // 2
            rows = pl.ds(pl.multiple_of(c * n, n), n)
            buf[3, rows] = (d1[...].astype(F32) + d2[...].astype(F32)) * 0.25
            fx[k + "s"] = push(buf.at[3, rows], buf.at[3, rows], dev(dc=1))

    def frag_4():
        for k in "lr":
            fx[k + "s"].wait_recv()
        return [local(fl.at[3], o_pl), local(fr.at[3], o_pr)]

    gx = {}

    def gout_1():
        lt = low[...].T.astype(BF)
        for q in range(2):
            part = nn(lt, cotv[:, q * 512 : (q + 1) * 512]) * (ADAPTER_SCALE * shrink)
            go[q] = part.astype(BF).reshape(4, 4, 16, 512)
        for q in range(2):
            for k, d in enumerate((1, -1, 2)):
                o = mod4(pos[q][0] + d)
                src = go.at[0, o] if q == 0 else go.at[1, :, o]
                gx[q, 1, k] = push(src, go_o.at[q, k], out_dev(q, d))

    def gout_2():
        for q in range(2):
            for k in range(3):
                gx[q, 1, k].wait_recv()
            own = go[0, y] if q == 0 else go[1, :, z]
            total = own.astype(F32)
            for k in range(3):
                total = total + go_o[q, k].astype(F32)
            go_f[q] = total

    def gout_2s():
        for q in range(2):
            for k, d in enumerate((1, -1, 2)):
                i = mod4(pos[q][1] + d)
                gx[q, 2, k] = push(go_f.at[q, i], go_i.at[q, k], in_dev(q, d))

    def gout_3():
        for q in range(2):
            for k in range(3):
                gx[q, 2, k].wait_recv()
            total = go_f[q, pos[q][1]]
            for k in range(3):
                total = total + go_i[q, k]
            go_x[:, :, q * 512 : (q + 1) * 512] = total.reshape(2, 8, 512)
        gx["x"] = push(go_x.at[xl1], gout.at[1], xpair())

    def gout_4():
        gx["x"].wait_recv()
        gout[0] = go_x[xl] + gout[1]
        return [local(gout.at[0], o_gout)]

    outs = []

    def finish(ch):
        cols = slice(ch * 512, (ch + 1) * 512)
        lowb = low[...].astype(BF)
        sums = jnp.zeros((1, 512), F32)
        for k in range(3):
            rows = slice(k * 256, (k + 1) * 256)
            fo = acc[ch, rows]
            mix = fo * scalev[:, cols] + ADAPTER_SCALE * nn(lowb[rows], upv[:, cols])
            val[rows, cols] = mix.astype(BF)
            sums = sums + jnp.sum(cotv[rows, cols].astype(F32) * fo, axis=0, keepdims=True)
        gs[0:1, cols] = sums * shrink

    sx = {}

    def scale_x():
        sx["x"] = push(gs.at[0:1], gs_o.at[6:7], xpair())

    def scale_i():
        sx["x"].wait_recv()
        gs[1:2] = gs[0:1] + gs_o[6:7]
        for k, d in enumerate((1, -1, 2)):
            sx["i", k] = push(gs.at[1:2], gs_o.at[k : k + 1], dev(dz=d))

    def scale_o():
        for k in range(3):
            sx["i", k].wait_recv()
        gs[2:3] = (gs[1:2] + gs_o[2:3]) + (gs_o[0:1] + gs_o[1:2])
        for k, d in enumerate((1, -1, 2)):
            sx["o", k] = push(gs.at[2:3], gs_o.at[3 + k : 4 + k], dev(dy=d))

    def scale_f():
        for k in range(3):
            sx["o", k].wait_recv()
        gs[3:4] = (gs[2:3] + gs_o[5:6]) + (gs_o[3:4] + gs_o[4:5])
        return [local(gs.at[3:4], o_gs)]

    def both(fn):
        fn(0)
        fn(1)

    both(w_in1)
    a_x1()
    back()
    both(w_in2)
    grad_in([0, 1])
    both(w_out1)
    both(a_in1)
    grad_in([2, 3, 4, 5, 6, 7])
    both(a_in2)
    ld_s.wait()
    outs += frag_1()
    both(rs_1)
    rotate(0, 8)
    frag_2()
    both(a_out1)
    both(w_out2)
    rotate(8, 16)
    both(rs_2)
    for q in range(2):
        w_sib[q][0, 0].wait_recv()
        for ch in range(2):
            frozen(q, xl, 0, ch, first=q == 0)
    frag_3()
    both(a_out2)
    both(w_out3)
    for q in range(2):
        for d in (1, -1):
            w_sib[q][0, d].wait_recv()
            for ch in range(2):
                frozen(q, xl, d, ch)
    for q in range(2):
        w_x1(q, 0)
    both(a_out3)
    low_rank()
    gout_1()
    both(rs_3)
    both(rs_4)
    for q in range(2):
        w_sib[q][0, 2].wait_recv()
        for ch in range(2):
            frozen(q, xl, 2, ch)
    gout_2()
    gout_2s()
    both(rs_5)
    outs += frag_4()
    for d in (1, -1):
        for q in range(2):
            w_x1(q, d)
    for q in range(2):
        w_sib[q][1, 0].wait_recv()
        for ch in range(2):
            frozen(q, xl1, 0, ch)
    gout_3()
    both(rs_6)
    for d in (1, -1):
        for q in range(2):
            w_sib[q][1, d].wait_recv()
            for ch in range(2):
                frozen(q, xl1, d, ch)
    outs += gout_4()
    for q in range(2):
        w_x1(q, 2)
    for q in range(2):
        w_sib[q][1, 2].wait_recv()
        for ch in range(2):
            frozen(q, xl1, 2, ch)
    ld_sc.wait()
    for ch in range(2):
        finish(ch)
    scale_x()
    outs.append(local(val, o_val))
    both(rs_7)
    scale_i()
    outs.append(local(gin, o_gin))
    scale_o()
    outs += scale_f()
    for cp in sent:
        cp.wait_send()
    for cp in outs:
        cp.wait()


def call(*args):
    vm = pltpu.VMEM
    out = [
        jax.ShapeDtypeStruct((ROWS, 1024), BF),
        jax.ShapeDtypeStruct((256, 256), F32),
        jax.ShapeDtypeStruct((8, 1024), F32),
        jax.ShapeDtypeStruct((1, 1024), F32),
        jax.ShapeDtypeStruct((1024, 256), F32),
        jax.ShapeDtypeStruct((32, 1024), F32),
        jax.ShapeDtypeStruct((1024, 256), F32),
        jax.ShapeDtypeStruct((32, 1024), F32),
        jax.ShapeDtypeStruct((1024, 256), F32),
        jax.ShapeDtypeStruct((32, 1024), F32),
    ]
    scratch = [
        vm((2, 2, 2, 4, 4, 128, 512), BF),
        vm((4, 4, 2, 2, 128, 256), BF),
        vm((ROWS, 8192), BF),
        vm((2, 48, 8192), BF),
        vm((2, ROWS, 512), BF),
        vm((4, 4, 2, 2, 128, 256), BF),
        vm((2, 2, 2, 2, 128, 256), BF),
        vm((2, 2, 4, 2, 128, 256), BF),
        vm((2, 2, 128, 256), BF),
        vm((2, 2, 2, 128, 256), BF),
        vm((2, 128, 256), BF),
        vm((ROWS, 1024), BF),
        vm((256, 1024), BF),
        vm((2, ROWS, 512), F32),
        vm((ROWS, 256), F32),
        vm((256, ROWS), BF),
        vm((ROWS, 1024), BF),
        vm((1, 8192), F32),
        vm((1, 1024), F32),
        vm((256, 256), BF),
        vm((256, 512), BF),
        vm((2, 4, 4, 16, 512), BF),
        vm((2, 3, 4, 16, 512), BF),
        vm((2, 3, 16, 512), F32),
        vm((2, 8, 1024), F32),
        vm((2, 4, 16, 512), F32),
        vm((8, 1024), F32),
        vm((8, 1024), F32),
        vm((4, 1024, 256), F32),
        vm((4, 32, 1024), F32),
        vm((2, 512, 256), BF),
        vm((2, 16, 1024), BF),
        vm((512, 256), BF),
        vm((16, 1024), BF),
        vm((512, 256), BF),
        vm((16, 1024), BF),
        vm((256, 256), F32),
        vm((2, 8, 1024), F32),
        pltpu.SemaphoreType.DMA((NSEM,)),
        pltpu.SemaphoreType.DMA((NSEM,)),
        pltpu.SemaphoreType.DMA((40,)),
        pltpu.SemaphoreType.DMA((2,)),
        pltpu.SemaphoreType.DMA((2,)),
    ]
    hbm = pl.BlockSpec(memory_space=pl.ANY)
    return pl.pallas_call(
        body,
        name="step",
        out_shape=out,
        in_specs=[hbm] * len(args),
        out_specs=[hbm] * len(out),
        scratch_shapes=scratch,
        compiler_params=pltpu.CompilerParams(
            collective_id=0, has_side_effects=True, vmem_limit_bytes=64 * 1024 * 1024
        ),
        cost_estimate=pl.CostEstimate(flops=23_000_000_000, bytes_accessed=30_000_000, transcendentals=0),
    )(*args)


def per_device(
    tokens, sign_bits, base_weight, learned_column_scale, adapter_in, adapter_up_weight, out_cotangent,
    local_left, local_right, global_left, global_right, moment_left, moment_right, pending_left, pending_right,
):
    sign = (1 - 2 * sign_bits).astype(F32).reshape(1, 8192)
    left = [a.reshape(1024, 256) for a in (local_left, global_left, moment_left, pending_left)]
    right = [a.reshape(32, 1024) for a in (local_right, global_right, moment_right, pending_right)]
    pairs = [a for pair in zip(left, right) for a in pair]
    had = jnp.asarray(hadamard(256), BF)
    out = call(
        tokens, sign, base_weight, learned_column_scale.reshape(1, 1024),
        adapter_in.reshape(2, 128, 256), adapter_up_weight.reshape(256, 1024), out_cotangent, *pairs, had,
    )
    val, gin, gout, gs, gl, gr, ml, mr, pdl, pdr = out
    return (
        val, gin[None], gout[None], gs,
        gl.reshape(4, 256, 256), gr.reshape(4, 8, 1024), ml.reshape(4, 256, 256), mr.reshape(4, 8, 1024),
        pdl.reshape(4, 256, 256), pdr.reshape(4, 8, 1024),
    )


def solution(mesh):
    rows, frag = P(("replica", "fsdp"), None), P(None, "fsdp", None)
    return jax.shard_map(
        per_device,
        mesh=mesh,
        in_specs=(
            rows, P(), P("fsdp", None), P(), P("replica", "fsdp", None), P("replica", None, None), rows,
            P("replica", None, "fsdp", None), P("replica", None, "fsdp", None),
        ) + (frag,) * 6,
        out_specs=(rows, P("replica", "fsdp", None), P("replica", "fsdp", None), P("replica", None)) + (frag,) * 6,
        check_vma=False,
    )
```

time: 919 us -> 137 us (0.15)
  waiting for transfers between devices: 740 us -> 0 us
  Pallas kernels: 0 us -> 123 us
  blocking collectives: 78.8 us -> 0 us
  matrix products: 60.2 us -> 0 us
  between operations: 15.8 us -> 0.69 us
  other arithmetic: 15.7 us -> 1.38 us
    all_gather x2 -> x0, waiting for transfers between devices: 482 us -> none  [the longest x1 362 us: per_device(): lax.all_gather(base_weight, 'fsdp', axis=0, tiled=True)]
    reduce_scatter x2 -> x0, waiting for transfers between devices: 246 us -> none  [the longest x1 187 us: per_device(): lax.psum_scatter(lax.dot_general(tokens, backward_rank_term, (((0,), (0,)...]
    pallas_call x0 -> x1, Pallas kernels: none -> 123 us  [call(): pl.pallas_call(body, name='step', out_shape=out, in_specs=[hbm] * len(arg...]
    psum x1 -> x0, blocking collectives: 78.8 us -> none  [per_device(): lax.psum(jnp.sum(output_gradient * frozen_output, axis=0) * shrink_factor...]
    dot_general x6 -> x0, matrix products: 60.2 us -> none  [the longest x1 21.4 us: per_device(): jnp.dot(rotated, lax.all_gather(base_weight, 'fsdp', axis=0, tiled=True),...]
    psum x1 -> x0, waiting for transfers between devices: 10.8 us -> none  [fragment_step(): lax.psum((global_left - local_left[0]).astype(jnp.bfloat16), 'replica')]
  transfers between devices with their start and end apart: 5 -> 0, of which waited for: 5 -> 0; matrix products, arithmetic and copies ran while one was open for 9% -> 0% of each run, Pallas kernels for 0% -> 0%
where the time goes in v1:
time: 137 us; the launch traced here: 135 us
  Pallas kernels  123 us (90%)
  local copies, waits for them, and re-layouts  9.59 us (7%)
  other arithmetic  1.38 us (1%)
    pallas_call x1, Pallas kernels, call(): pl.pallas_call(body, name='step', out_shape=out, in_specs=[hbm] * len(arg...  123 us
    unnamed x28, local copies, waits for them, and re-layouts  9.59 us

profile of v1, /device:TPU:0, one launch (start us, length us, event | category | flops | bytes accessed | tf_op | source)
XLA Modules:
  0.0 135.1 jit_solution(4718469238888089019)
XLA Ops:
  0.6 1.4 %subtract_convert_fusion = f32[8192]{0:T(1024)} fusion(s32[8192]{0:T(1024)} %param.17), kind=kLoop, calls=%fused_computation | loop fusion | flops 24576 | bytes 65536 | tf_op jit(solution)/shard_map/convert_element_type | solution.py:642
  2.0 123.4 %step.1 = (bf16[768,1024]{1,0:T(8,128)(2,1)}, f32[256,256]{1,0:T(8,128)}, f32[8,1024]{1,0:T(8,128)}, f32[1,1024]{1,0:T(1,128)}, f32[1024,256]{1,0:T(8,128)}, /*i...) custom-call(bf16[768,8192]{1,0:T(8,128)(2,1)} %tokens.1, ...), custom_call_target="tpu_custom_call" | custom-call | flops 23000000512 | bytes 30000000 | tf_op jit(solution)/shard_map/step/pallas_call | solution.py:624
  125.5 0.0 copy-start.3
  125.5 0.0 copy-start.7
  125.5 0.0 copy-start.8
  125.5 0.0 copy-start.2
  125.5 2.8 %copy.36 = bf16[768,1024]{1,0:T(8,128)(2,1)} copy(bf16[768,1024]{1,0:T(8,128)(2,1)} %get-tuple-element.40) | data formatting | bytes 3145728
  128.3 0.0 copy-done.3
  128.3 0.0 copy-start.6
  128.3 0.0 copy-start.1
  128.3 0.7 copy.37
  129.0 0.0 copy-done.7
  129.0 0.6 copy.38
  129.6 0.0 copy-done.8
  129.6 0.6 copy.39
  130.2 0.0 copy-done.2
  130.2 1.0 copy.40
  131.2 0.0 copy-done.6
  131.2 0.0 copy-start.5
  131.2 0.0 copy-start
  131.2 0.7 copy.41
  131.8 0.0 copy-done.1
  131.8 1.0 copy.42
  132.8 0.0 copy-done.5
  132.8 0.0 copy-start.4
  132.8 0.7 copy.43
  133.5 0.0 copy-done
  133.5 1.0 copy.44
  134.4 0.0 copy-done.4
  134.4 0.7 copy.45
Async XLA Ops:
  125.5 2.8 %copy-start.3 = (f32[256,256]{1,0:T(8,128)S(1)}, f32[256,256]{1,0:T(8,128)}, u32[]{:S(2)}) copy-start(f32[256,256]{1,0:T(8,128)} %get-tuple-element.21) | copy-start | bytes 786436
  125.5 3.5 %copy-start.7 = (f32[8,1024]{1,0:T(8,128)S(1)}, f32[8,1024]{1,0:T(8,128)}, u32[]{:S(2)}) copy-start(f32[8,1024]{1,0:T(8,128)} %get-tuple-element.22) | copy-start | bytes 98308
  125.5 4.1 %copy-start.8 = (f32[1,1024]{1,0:T(1,128)S(1)}, f32[1,1024]{1,0:T(1,128)}, u32[]{:S(2)}) copy-start(f32[1,1024]{1,0:T(1,128)} %get-tuple-element.43) | copy-start | bytes 12292
  125.5 4.7 %copy-start.2 = (f32[1024,256]{1,0:T(8,128)S(1)}, f32[1024,256]{1,0:T(8,128)}, u32[]{:S(2)}) copy-start(f32[1024,256]{1,0:T(8,128)} %get-tuple-element.24) | copy-start | bytes 3145732
  128.3 2.9 %copy-start.6 = (f32[32,1024]{1,0:T(8,128)S(1)}, f32[32,1024]{1,0:T(8,128)}, u32[]{:S(2)}) copy-start(f32[32,1024]{1,0:T(8,128)} %get-tuple-element.25) | copy-start | bytes 393220
  128.3 3.6 %copy-start.1 = (f32[1024,256]{1,0:T(8,128)S(1)}, f32[1024,256]{1,0:T(8,128)}, u32[]{:S(2)}) copy-start(f32[1024,256]{1,0:T(8,128)} %get-tuple-element.26) | copy-start | bytes 3145732
  131.2 1.6 %copy-start.5 = (f32[32,1024]{1,0:T(8,128)S(1)}, f32[32,1024]{1,0:T(8,128)}, u32[]{:S(2)}) copy-start(f32[32,1024]{1,0:T(8,128)} %get-tuple-element.27) | copy-start | bytes 393220
  131.2 2.3 %copy-start = (f32[1024,256]{1,0:T(8,128)S(1)}, f32[1024,256]{1,0:T(8,128)}, u32[]{:S(2)}) copy-start(f32[1024,256]{1,0:T(8,128)} %get-tuple-element.28) | copy-start | bytes 3145732
  132.8 1.6 %copy-start.4 = (f32[32,1024]{1,0:T(8,128)S(1)}, f32[32,1024]{1,0:T(8,128)}, u32[]{:S(2)}) copy-start(f32[32,1024]{1,0:T(8,128)} %get-tuple-element.29) | copy-start | bytes 393220

commit v2 on v1

--- a/solution.py
+++ b/solution.py
@@ -2,7 +2,6 @@
 
 import jax
 import jax.numpy as jnp
-import numpy as np
 from jax import lax
 from jax.experimental import pallas as pl
 from jax.experimental.pallas import tpu as pltpu
@@ -15,16 +14,7 @@
 MOMENTUM = 0.9
 OUTER_RATE = 0.7
 ROWS = 768
-NSEM = 160
-
-
-def hadamard(n):
-    i = np.arange(n)
-    both = i[:, None] & i[None, :]
-    parity = np.zeros((n, n), np.int64)
-    for b in range(n.bit_length()):
-        parity += (both >> b) & 1
-    return (1 - 2 * (parity % 2)).astype(np.float32)
+NSEM = 192
 
 
 def nt(a, b):
@@ -36,11 +26,11 @@
 
 
 def body(
-    tokens, sign, weight, scale, a_in, up, cot, ll, lr, gl, gr, ml, mr, pend_l, pend_r, had,
+    tokens, sign, weight, scale, a_in, up, cot, ll, lr, gl, gr, ml, mr, pend_l, pend_r,
     o_val, o_gin, o_gout, o_gs, o_gl, o_gr, o_ml, o_mr, o_pl, o_pr,
-    wg, ag, tok, st, sl, g, r1, r2, r3, r4, r5, cotv, upv, acc, low, bt, val, signv, scalev, hadv, wsh,
+    wg, ag, tok, st, sgn, sl, g, r1, r2, r3, r4, r5, cotv, upv, acc, low, bt, val, signv, scalev, wsh,
     go, go_o, go_i, go_x, go_f, gs, gs_o, fl, fr, dl, dr, dl1, dr1, dl2, dr2, gin, gout,
-    send, recv, loc, st_sem, sl_sem,
+    send, recv, loc, sl_sem,
 ):
     r, f = lax.axis_index("replica"), lax.axis_index("fsdp")
     xh, c = r // 2, r % 2
@@ -80,22 +70,20 @@
         sent.append(cp)
         return cp
 
-    def row_copy(k):
-        rows = pl.ds(pl.multiple_of(k * 48, 48), 48)
-        return pltpu.make_async_copy(tokens.at[rows], st.at[k % 2], st_sem.at[k % 2])
-
-    def col_copy(k):
-        cols = pl.ds(pl.multiple_of(k * 512, 512), 512)
-        return pltpu.make_async_copy(tokens.at[:, cols], sl.at[k % 2], sl_sem.at[k % 2])
+    def col_copies(k):
+        cols = pl.ds(pl.multiple_of(k * 1024, 1024), 1024)
+        return [
+            pltpu.make_async_copy(
+                tokens.at[pl.ds(n * 192, 192), cols], sl.at[k % 2, pl.ds(n * 192, 192)], sl_sem.at[k % 2, n]
+            )
+            for n in range(4)
+        ]
 
     ld_w = local(weight.at[:, pl.ds(pl.multiple_of(c * 512, 512), 512)], wsh)
-    ld_h = local(had, hadv)
     ld_a = local(a_in, ag.at[y, z, xl])
     ld_up = local(up, upv)
     ld_cot = local(cot, cotv)
     ld_tok = [local(tokens.at[:, pl.ds(k * 1024, 1024)], tok.at[:, pl.ds(k * 1024, 1024)]) for k in range(8)]
-    row_copy(0).start()
-    col_copy(0).start()
     ld_s = local(sign, signv)
     ld_sc = local(scale, scalev)
     ld_f = [local(s, fl.at[k]) for k, s in enumerate((ll, gl, ml, pend_l))]
@@ -107,8 +95,11 @@
         pl.semaphore_signal(barrier, inc=1, device_id=p, device_id_type=MESH)
 
     ld_w.wait()
-    ld_h.wait()
-    w1 = (nn(hadv[...], wsh[...]) * (1.0 / math.sqrt(8192))).astype(BF)
+    both_bits = lax.broadcasted_iota(jnp.int32, (256, 256), 0) & lax.broadcasted_iota(jnp.int32, (256, 256), 1)
+    for b in (4, 2, 1):
+        both_bits = both_bits ^ (both_bits >> b)
+    had = (1 - 2 * (both_bits & 1)).astype(F32).astype(BF)
+    w1 = (nn(had, wsh[...]) * (1.0 / math.sqrt(8192))).astype(BF)
     wg[c, 0, xl, y, z] = w1[:128]
     wg[c, 1, xl, z, y] = w1[128:]
     pl.semaphore_wait(barrier, len(peers))
@@ -121,54 +112,83 @@
     def in_dev(q, d):
         return dev(dz=d) if q == 0 else dev(dy=d)
 
-    w_in, w_out, w_x, w_sib = [{}, {}], [{}, {}], [{}, {}], [{}, {}]
-
-    def wgrp(q, xv, d, ch=None):
-        return wg.at[c if ch is None else ch, q, xv, mod4(pos[q][0] + d)]
-
-    def w_in1(q):
+    w_in, w_po, w_pf, w_px, w_sib = ([{}, {}] for _ in range(5))
+
+    def wp(q, do, di):
         o, i = pos[q]
-        ref = wg.at[c, q, xl, o, i]
+        return wg.at[c, q, xl, mod4(o + do), mod4(i + di)]
+
+    def x_dev(q):
+        return dev(dx=-1 if q == 0 else 1)
+
+    def w_out(q, di):
+        ref = wp(q, 0, di)
+        for d in (1, -1):
+            w_po[q][di, d] = push(ref, ref, out_dev(q, d))
+
+    def w_cross(q, do, di):
+        ref = wp(q, do, di)
+        w_px[q][do, di] = push(ref, ref, x_dev(q))
+
+    def w_share(q, far, do):
+        ref = wg.at[c, q, xl1 if far else xl, mod4(pos[q][0] + do)]
+        w_sib[q][far, do] = push(ref, ref, dev(dc=1))
+
+    def w_1(q):
+        ref = wp(q, 0, 0)
         for d in (1, -1):
             w_in[q][d] = push(ref, ref, in_dev(q, d))
-
-    def w_in2(q):
-        o, i = pos[q]
+        w_out(q, 0)
+        w_cross(q, 0, 0)
+
+    def w_2(q):
         for d, h in ((1, 0), (-1, 64)):
             w_in[q][d].wait_recv()
+            o, i = pos[q]
             ref = wg.at[c, q, xl, o, mod4(i - d), pl.ds(h, 64)]
             w_in[q][2 * d] = push(ref, ref, in_dev(q, d))
-
-    def w_share(q, d):
-        ref = wgrp(q, xl, d)
-        w_x[q][d] = push(ref, ref, dev(dx=-1 if q == 0 else 1))
-        w_sib[q][0, d] = push(ref, ref, dev(dc=1))
-
-    def w_out1(q):
+            w_out(q, -d)
+            w_cross(q, 0, -d)
+
+    def w_fwd(q, d, di):
+        ref = wp(q, -d, di)
+        w_pf[q][di] = push(ref, ref, out_dev(q, d))
+
+    def w_got(q, d, di):
+        w_po[q][di, d].wait_recv()
+        w_cross(q, -d, di)
+        if (d == 1) == (di in (0, 1)):
+            w_fwd(q, d, di)
+
+    def w_3(q):
+        for d in (1, -1):
+            w_got(q, d, 0)
         for d in (1, -1):
             w_in[q][2 * d].wait_recv()
-        ref = wgrp(q, xl, 0)
-        for d in (1, -1):
-            w_out[q][d] = push(ref, ref, out_dev(q, d))
-        w_share(q, 0)
-
-    def w_out2(q):
-        for d, h in ((1, 0), (-1, 2)):
-            w_out[q][d].wait_recv()
-            ref = wg.at[c, q, xl, mod4(pos[q][0] - d), pl.ds(h, 2)]
-            w_out[q][2 * d] = push(ref, ref, out_dev(q, d))
-        for d in (1, -1):
-            w_share(q, d)
-
-    def w_out3(q):
-        for d in (1, -1):
-            w_out[q][2 * d].wait_recv()
-        w_share(q, 2)
-
-    def w_x1(q, d):
-        w_x[q][d].wait_recv()
-        ref = wgrp(q, xl1, d)
-        w_sib[q][1, d] = push(ref, ref, dev(dc=1))
+        w_out(q, 2)
+        w_cross(q, 0, 2)
+        w_share(q, 0, 0)
+
+    def w_4(q):
+        for di in (1, -1):
+            for d in (1, -1):
+                w_got(q, d, di)
+
+    def w_5(q):
+        for d in (1, -1):
+            w_got(q, d, 2)
+            w_share(q, 0, -d)
+
+    def w_6(q):
+        for di in (0, 1, -1, 2):
+            w_pf[q][di].wait_recv()
+            w_cross(q, 2, di)
+        w_share(q, 0, 2)
+
+    def w_7(q, do):
+        for di in (0, 1, -1, 2):
+            w_px[q][do, di].wait_recv()
+        w_share(q, 1, do)
 
     a_x, a_i, a_o = {}, [{}, {}], [{}, {}]
 
@@ -292,46 +312,45 @@
             ld_tok[k].wait()
 
         def one(j, carry):
-            cols = pl.ds(pl.multiple_of(j * 256, 256), 256)
+            cols = pl.ds(pl.multiple_of(j * 1024, 1024), 1024)
             part = nn(bt[...], tok[:, cols]).astype(BF)
-            g[j // 8, (j // 2) % 4, j % 2, 0] = part[:128]
-            g[j // 8, (j // 2) % 4, j % 2, 1] = part[128:]
+            for n in range(4):
+                for q in range(2):
+                    g[j // 2, (j % 2) * 2 + n // 2, n % 2, q] = part[q * 128 : q * 128 + 128, n * 256 : n * 256 + 256]
             return carry
 
-        lax.fori_loop(ks[0] * 4, ks[-1] * 4 + 4, one, 0)
+        lax.fori_loop(ks[0], ks[-1] + 1, one, 0)
+
+    def signs():
+        ld_s.wait()
+
+        def one(k, carry):
+            cols = pl.ds(pl.multiple_of(k * 1024, 1024), 1024)
+            flip = (1 - 2 * signv[:, cols]).astype(F32)
+            sgn[:, cols] = jnp.broadcast_to(flip, (16, 1024)).astype(BF)
+            return carry
+
+        lax.fori_loop(0, 8, one, 0)
 
     def rotate(lo, hi):
-        def chunk(k, carry):
-            row_copy(k).wait()
-
-            @pl.when(k + 1 < 16)
-            def _():
-                row_copy(k + 1).start()
-
-            lax.fori_loop(0, 6, lambda j, n: rotate_rows(k, j, n), 0)
+        def one(k, carry):
+            rows = pl.ds(pl.multiple_of(k * 16, 16), 16)
+            st[...] = tok[rows] * sgn[...]
+            for q in range(2):
+                parts = [st[:, j * 256 + q * 128 : j * 256 + q * 128 + 128] for j in range(32)]
+                for b in range(5):
+                    step = 1 << b
+                    for j in range(32):
+                        if not j & step:
+                            u, v = parts[j], parts[j + step]
+                            parts[j], parts[j + step] = u + v, u - v
+                for j in range(32):
+                    jy, jz, jx = j // 8, (j // 2) % 4, j % 2
+                    t = q * 32 + jx * 16 + (1 - q) * (jy * 4 + jz) + q * (jz * 4 + jy)
+                    tok[rows, t * 128 : t * 128 + 128] = parts[j]
             return carry
 
-        lax.fori_loop(lo, hi, chunk, 0)
-
-    def rotate_rows(chunk, k, carry):
-        at = pl.multiple_of((k // 2) * 16, 16)
-        rows = pl.ds(pl.multiple_of(chunk * 48 + at, 16), 16)
-        q = k % 2
-        parts = []
-        for j in range(32):
-            cols = pl.ds(pl.multiple_of(j * 256 + q * 128, 128), 128)
-            parts.append(st[chunk % 2, pl.ds(at, 16), cols].astype(F32) * signv[:, cols])
-        for b in range(5):
-            step = 1 << b
-            for j in range(32):
-                if not j & step:
-                    u, v = parts[j], parts[j + step]
-                    parts[j], parts[j + step] = u + v, u - v
-        for j in range(32):
-            jy, jz, jx = j // 8, (j // 2) % 4, j % 2
-            t = q * 32 + jx * 16 + (1 - q) * (jy * 4 + jz) + q * (jz * 4 + jy)
-            tok[rows, pl.ds(pl.multiple_of(t * 128, 128), 128)] = parts[j].astype(BF)
-        return carry
+        lax.fori_loop(lo, hi, one, 0)
 
     def frozen(q, xv, d, ch, first=False):
         o = mod4(pos[q][0] + d)
@@ -342,19 +361,25 @@
         else:
             acc[ch] += part
 
-    def low_rank():
+    def low_start():
+        for cp in col_copies(0) + col_copies(1):
+            cp.start()
+
+    def low_rank(lo, hi):
         def one(k, carry):
-            col_copy(k).wait()
-
-            @pl.when(k + 1 < 16)
+            for cp in col_copies(k):
+                cp.wait()
+            part = nn(sl[k % 2], ag[k // 2, pl.ds((k % 2) * 2, 2)].reshape(1024, 256))
+            low[...] = jnp.where(k == 0, part, low[...] + part)
+
+            @pl.when(k + 2 < 8)
             def _():
-                col_copy(k + 1).start()
-
-            part = nn(sl[k % 2], ag[k // 4, k % 4].reshape(512, 256))
-            low[...] = jnp.where(k == 0, part, low[...] + part)
+                for cp in col_copies(k + 2):
+                    cp.start()
+
             return carry
 
-        lax.fori_loop(0, 16, one, 0)
+        lax.fori_loop(lo, hi, one, 0)
 
     fx = {}
 
@@ -479,81 +504,72 @@
         fn(0)
         fn(1)
 
-    both(w_in1)
+    def use(far, do):
+        for q in range(2):
+            w_sib[q][far, do].wait_recv()
+            for ch in range(2):
+                frozen(q, xl1 if far else xl, do, ch, first=far == 0 and do == 0 and q == 0)
+
+    both(w_1)
     a_x1()
     back()
-    both(w_in2)
     grad_in([0, 1])
-    both(w_out1)
+    both(w_2)
+    grad_in([2, 3, 4, 5])
     both(a_in1)
-    grad_in([2, 3, 4, 5, 6, 7])
+    both(w_3)
+    grad_in([6, 7])
+    signs()
+    rotate(0, 24)
+    both(w_4)
     both(a_in2)
-    ld_s.wait()
+    rotate(24, 48)
+    both(w_5)
+    both(a_out1)
+    low_start()
     outs += frag_1()
+    use(0, 0)
+    both(w_6)
     both(rs_1)
-    rotate(0, 8)
+    use(0, 1)
+    use(0, -1)
+    for q in range(2):
+        w_7(q, 0)
     frag_2()
-    both(a_out1)
-    both(w_out2)
-    rotate(8, 16)
+    use(0, 2)
+    both(a_out2)
+    use(1, 0)
     both(rs_2)
-    for q in range(2):
-        w_sib[q][0, 0].wait_recv()
-        for ch in range(2):
-            frozen(q, xl, 0, ch, first=q == 0)
-    frag_3()
-    both(a_out2)
-    both(w_out3)
-    for q in range(2):
-        for d in (1, -1):
-            w_sib[q][0, d].wait_recv()
-            for ch in range(2):
-                frozen(q, xl, d, ch)
-    for q in range(2):
-        w_x1(q, 0)
+    for do in (1, -1):
+        for q in range(2):
+            w_7(q, do)
     both(a_out3)
-    low_rank()
+    low_rank(0, 8)
     gout_1()
     both(rs_3)
     both(rs_4)
-    for q in range(2):
-        w_sib[q][0, 2].wait_recv()
-        for ch in range(2):
-            frozen(q, xl, 2, ch)
+    use(1, 1)
+    use(1, -1)
+    frag_3()
     gout_2()
     gout_2s()
     both(rs_5)
+    for q in range(2):
+        w_7(q, 2)
+    both(rs_6)
     outs += frag_4()
-    for d in (1, -1):
-        for q in range(2):
-            w_x1(q, d)
-    for q in range(2):
-        w_sib[q][1, 0].wait_recv()
-        for ch in range(2):
-            frozen(q, xl1, 0, ch)
-    gout_3()
-    both(rs_6)
-    for d in (1, -1):
-        for q in range(2):
-            w_sib[q][1, d].wait_recv()
-            for ch in range(2):
-                frozen(q, xl1, d, ch)
-    outs += gout_4()
-    for q in range(2):
-        w_x1(q, 2)
-    for q in range(2):
-        w_sib[q][1, 2].wait_recv()
-        for ch in range(2):
-            frozen(q, xl1, 2, ch)
+    use(1, 2)
     ld_sc.wait()
     for ch in range(2):
         finish(ch)
     scale_x()
     outs.append(local(val, o_val))
+    gout_3()
+    scale_i()
     both(rs_7)
-    scale_i()
     outs.append(local(gin, o_gin))
     scale_o()
+    outs += gout_4()
     outs += scale_f()
     for cp in sent:
         cp.wait_send()
@@ -579,8 +595,9 @@
         vm((2, 2, 2, 4, 4, 128, 512), BF),
         vm((4, 4, 2, 2, 128, 256), BF),
         vm((ROWS, 8192), BF),
-        vm((2, 48, 8192), BF),
-        vm((2, ROWS, 512), BF),
+        vm((16, 8192), BF),
+        vm((16, 8192), BF),
+        vm((2, ROWS, 1024), BF),
         vm((4, 4, 2, 2, 128, 256), BF),
         vm((2, 2, 2, 2, 128, 256), BF),
         vm((2, 2, 4, 2, 128, 256), BF),
@@ -593,9 +610,8 @@
         vm((ROWS, 256), F32),
         vm((256, ROWS), BF),
         vm((ROWS, 1024), BF),
-        vm((1, 8192), F32),
+        vm((1, 8192), jnp.int32),
         vm((1, 1024), F32),
-        vm((256, 256), BF),
         vm((256, 512), BF),
         vm((2, 4, 4, 16, 512), BF),
         vm((2, 3, 4, 16, 512), BF),
@@ -617,8 +633,7 @@
         pltpu.SemaphoreType.DMA((NSEM,)),
         pltpu.SemaphoreType.DMA((NSEM,)),
         pltpu.SemaphoreType.DMA((40,)),
-        pltpu.SemaphoreType.DMA((2,)),
-        pltpu.SemaphoreType.DMA((2,)),
+        pltpu.SemaphoreType.DMA((2, 4)),
     ]
     hbm = pl.BlockSpec(memory_space=pl.ANY)
     return pl.pallas_call(
@@ -635,25 +650,52 @@
     )(*args)
 
 
+def hand_over(refs):
+    n = len(refs)
+
+    def copy_all(*args):
+        src, dst, held = args[:n], args[n : 2 * n], args[2 * n : 3 * n]
+        sem_in, sem_out = args[3 * n :]
+        into = [pltpu.make_async_copy(a, b, sem_in.at[k]) for k, (a, b) in enumerate(zip(src, held))]
+        away = [pltpu.make_async_copy(a, b, sem_out.at[k]) for k, (a, b) in enumerate(zip(held, dst))]
+        for cp in into:
+            cp.start()
+        for a, b in zip(into, away):
+            a.wait()
+            b.start()
+        for cp in away:
+            cp.wait()
+
+    hbm = pl.BlockSpec(memory_space=pl.ANY)
+    return pl.pallas_call(
+        copy_all,
+        name="hand_over",
+        out_shape=[jax.ShapeDtypeStruct(a.shape, a.dtype) for a in refs],
+        in_specs=[hbm] * n,
+        out_specs=[hbm] * n,
+        scratch_shapes=[pltpu.VMEM(a.shape, a.dtype) for a in refs]
+        + [pltpu.SemaphoreType.DMA((n,)), pltpu.SemaphoreType.DMA((n,))],
+        compiler_params=pltpu.CompilerParams(vmem_limit_bytes=60 * 1024 * 1024),
+    )(*refs)
+
+
 def per_device(
     tokens, sign_bits, base_weight, learned_column_scale, adapter_in, adapter_up_weight, out_cotangent,
     local_left, local_right, global_left, global_right, moment_left, moment_right, pending_left, pending_right,
 ):
-    sign = (1 - 2 * sign_bits).astype(F32).reshape(1, 8192)
     left = [a.reshape(1024, 256) for a in (local_left, global_left, moment_left, pending_left)]
     right = [a.reshape(32, 1024) for a in (local_right, global_right, moment_right, pending_right)]
     pairs = [a for pair in zip(left, right) for a in pair]
-    had = jnp.asarray(hadamard(256), BF)
     out = call(
-        tokens, sign, base_weight, learned_column_scale.reshape(1, 1024),
-        adapter_in.reshape(2, 128, 256), adapter_up_weight.reshape(256, 1024), out_cotangent, *pairs, had,
+        tokens, sign_bits.reshape(1, 8192), base_weight, learned_column_scale.reshape(1, 1024),
+        adapter_in.reshape(2, 128, 256), adapter_up_weight.reshape(256, 1024), out_cotangent, *pairs,
     )
     val, gin, gout, gs, gl, gr, ml, mr, pdl, pdr = out
-    return (
+    return hand_over((
         val, gin[None], gout[None], gs,
         gl.reshape(4, 256, 256), gr.reshape(4, 8, 1024), ml.reshape(4, 256, 256), mr.reshape(4, 8, 1024),
         pdl.reshape(4, 256, 256), pdr.reshape(4, 8, 1024),
-    )
+    ))
 
 
 def solution(mesh):

time: 137 us -> 104 us (0.76)
  Pallas kernels: 123 us -> 102 us
  local copies, waits for them, and re-layouts: 9.59 us -> 0 us
  other arithmetic: 1.38 us -> 0 us
    pallas_call x1, Pallas kernels: 123 us -> 98.2 us  [call(): pl.pallas_call(body, name='step', out_shape=out, in_specs=[hbm] * len(arg...]
    unnamed x28 -> x0, local copies, waits for them, and re-layouts: 9.59 us -> none
    pallas_call x0 -> x1, Pallas kernels: none -> 4.09 us  [hand_over(): pl.pallas_call(copy_all, name='hand_over', out_shape=[jax.ShapeDtypeStruc...]
    convert_element_type x1 -> x0, other arithmetic: 1.38 us -> none  [per_device(): sign = (1 - 2 * sign_bits).astype(F32).reshape(1, 8192)]
where the time goes in v2:
time: 104 us; the launch traced here: 103 us
  Pallas kernels  102 us (98%)
    pallas_call x1, Pallas kernels, call(): pl.pallas_call(body, name='step', out_shape=out, in_specs=[hbm] * len(arg...  98.2 us
    pallas_call x1, Pallas kernels, hand_over(): pl.pallas_call(copy_all, name='hand_over', out_shape=[jax.ShapeDtypeStruc...  4.09 us

profile of v2, /device:TPU:0, one launch (start us, length us, event | category | flops | bytes accessed | tf_op | source)
XLA Modules:
  0.0 103.1 jit_solution(16415291738072926566)
XLA Ops:
  0.6 98.2 %step.1 = (bf16[768,1024]{1,0:T(8,128)(2,1)}, f32[256,256]{1,0:T(8,128)}, f32[8,1024]{1,0:T(8,128)}, f32[1,1024]{1,0:T(1,128)}, f32[1024,256]{1,0:T(8,128)}, /*i...) custom-call(bf16[768,8192]{1,0:T(8,128)(2,1)} %tokens.1, ...), custom_call_target="tpu_custom_call" | custom-call | flops 23000000512 | bytes 30000000 | tf_op jit(solution)/shard_map/step/pallas_call | solution.py:639
  98.9 4.1 %hand_over.1 = (bf16[768,1024]{1,0:T(8,128)(2,1)}, f32[1,256,256]{2,1,0:T(8,128)}, f32[1,8,1024]{2,1,0:T(8,128)}, f32[1,1024]{1,0:T(1,128)}, f32[4,256,256]{2,1,...) custom-call(bf16[768,1024]{1,0:T(8,128)(2,1)} %get-tuple-element.20., ...), custom_call_target="tpu_custom_call" | custom-call | tf_op jit(solution)/shard_map/hand_over/pallas_call | solution.py:670

commit v3 on v2

--- a/solution.py
+++ b/solution.py
@@ -14,7 +14,7 @@
 MOMENTUM = 0.9
 OUTER_RATE = 0.7
 ROWS = 768
-NSEM = 192
+NSEM = 224
 
 
 def nt(a, b):
@@ -29,7 +29,7 @@
     tokens, sign, weight, scale, a_in, up, cot, ll, lr, gl, gr, ml, mr, pend_l, pend_r,
     o_val, o_gin, o_gout, o_gs, o_gl, o_gr, o_ml, o_mr, o_pl, o_pr,
     wg, ag, tok, st, sgn, sl, g, r1, r2, r3, r4, r5, cotv, upv, acc, low, bt, val, signv, scalev, wsh,
-    go, go_o, go_i, go_x, go_f, gs, gs_o, fl, fr, dl, dr, dl1, dr1, dl2, dr2, gin, gout,
+    go, go_o, go_i, go_x, go_f, gs, gs_o, fl, fr, dl, dr, dl1, dr1, dl2, dr2, gin_t, gin, gout,
     send, recv, loc, sl_sem,
 ):
     r, f = lax.axis_index("replica"), lax.axis_index("fsdp")
@@ -47,6 +47,11 @@
 
     def mod4(v):
         return (v + 4) % 4
+
+    barrier = pltpu.get_barrier_semaphore()
+    peers = [dev(dx=1), dev(dx=-1), dev(dx=2), dev(dy=1), dev(dy=-1), dev(dy=2), dev(dz=1), dev(dz=-1), dev(dz=2), dev(dc=1)]
+    for p in peers:
+        pl.semaphore_signal(barrier, inc=1, device_id=p, device_id_type=MESH)
 
     nloc = [0]
 
@@ -70,8 +75,13 @@
         sent.append(cp)
         return cp
 
+    def low_chunk(k):
+        n = k % 4
+        return mod4(y + (n ^ (n // 2))), (z // 2 + k // 4) % 2
+
     def col_copies(k):
-        cols = pl.ds(pl.multiple_of(k * 1024, 1024), 1024)
+        cy, cz = low_chunk(k)
+        cols = pl.ds(pl.multiple_of(cy * 2048 + cz * 1024, 1024), 1024)
         return [
             pltpu.make_async_copy(
                 tokens.at[pl.ds(n * 192, 192), cols], sl.at[k % 2, pl.ds(n * 192, 192)], sl_sem.at[k % 2, n]
@@ -80,19 +90,14 @@
         ]
 
     ld_w = local(weight.at[:, pl.ds(pl.multiple_of(c * 512, 512), 512)], wsh)
+    ld_up = local(up, upv)
     ld_a = local(a_in, ag.at[y, z, xl])
-    ld_up = local(up, upv)
     ld_cot = local(cot, cotv)
     ld_tok = [local(tokens.at[:, pl.ds(k * 1024, 1024)], tok.at[:, pl.ds(k * 1024, 1024)]) for k in range(8)]
     ld_s = local(sign, signv)
     ld_sc = local(scale, scalev)
     ld_f = [local(s, fl.at[k]) for k, s in enumerate((ll, gl, ml, pend_l))]
     ld_f += [local(s, fr.at[k]) for k, s in enumerate((lr, gr, mr, pend_r))]
-
-    barrier = pltpu.get_barrier_semaphore()
-    peers = [dev(dx=1), dev(dx=-1), dev(dx=2), dev(dy=1), dev(dy=-1), dev(dy=2), dev(dz=1), dev(dz=-1), dev(dz=2), dev(dc=1)]
-    for p in peers:
-        pl.semaphore_signal(barrier, inc=1, device_id=p, device_id_type=MESH)
 
     ld_w.wait()
     both_bits = lax.broadcasted_iota(jnp.int32, (256, 256), 0) & lax.broadcasted_iota(jnp.int32, (256, 256), 1)
@@ -199,11 +204,11 @@
         return ag.at[o, i, :, 0] if q == 0 else ag.at[i, o, :, 1]
 
     def a_x1():
-        ld_a.wait()
-        a_x[0] = push(ag.at[y, z, xl], ag.at[y, z, xl], xpair())
+        a_x[0] = push(a_in, ag.at[y, z, xl], xpair())
 
     def a_in1(q):
         if q == 0:
+            ld_a.wait()
             a_x[0].wait_recv()
         ref = apiece(q, pos[q][1])
         for d in (1, -1):
@@ -232,74 +237,70 @@
         for d in (1, -1):
             a_o[q][2 * d].wait_recv()
 
-    rs = [{}, {}]
-
-    def gidx(q, o, i, xv):
-        return (o, i, xv, 0) if q == 0 else (i, o, xv, 1)
-
-    def ggrp(q, o, i=slice(None)):
-        return g.at[o, i, :, 0] if q == 0 else g.at[i, o, :, 1]
-
-    def add_to(q, o, i, xv, *terms):
-        at = gidx(q, o, i, xv)
+    rs = {}
+
+    def gat(q, t, o, i, xs):
+        return (o, i, xs, 2 * q + t) if q == 0 else (i, o, xs, 2 * q + t)
+
+    def gref(q, t, o, i, xs=slice(None)):
+        return g.at[gat(q, t, o, i, xs)]
+
+    def add_to(q, t, o, i, xv, *terms):
+        at = gat(q, t, o, i, xv)
         total = g[at].astype(F32)
-        for t in terms:
-            total = total + t.astype(F32)
+        for v in terms:
+            total = total + v.astype(F32)
         g[at] = total.astype(BF)
 
-    def rs_1(q):
+    def rs_1(q, t):
         o = mod4(pos[q][0] + 2)
         for k, (d, h) in enumerate(((1, 0), (-1, 2))):
-            rs[q][1, d] = push(ggrp(q, o, pl.ds(h, 2)), r1.at[q, k], out_dev(q, d))
-
-    def rs_2(q):
+            rs[q, t, 1, d] = push(gref(q, t, o, pl.ds(h, 2)), r1.at[2 * q + t, k], out_dev(q, d))
+
+    def rs_2(q, t):
         for k, (d, h) in enumerate(((1, 0), (-1, 2))):
-            rs[q][1, d].wait_recv()
+            rs[q, t, 1, d].wait_recv()
             o = mod4(pos[q][0] + d)
-
-            def one(j, carry, k=k, h=h, o=o):
-                add_to(q, o, h + j // 2, j % 2, r1[q, k, j // 2, j % 2])
-                return carry
-
-            lax.fori_loop(0, 4, one, 0)
-            rs[q][2, d] = push(ggrp(q, o), r2.at[q, k], out_dev(q, d))
-
-    def rs_3(q):
-        for d in (1, -1):
-            rs[q][2, d].wait_recv()
-
-        def one(j, carry):
-            add_to(q, pos[q][0], j // 2, j % 2, r2[q, 0, j // 2, j % 2], r2[q, 1, j // 2, j % 2])
-            return carry
-
-        lax.fori_loop(0, 8, one, 0)
-
-    def gpiece(q, i, xs=slice(None)):
-        return g.at[y, i, xs, 0] if q == 0 else g.at[i, z, xs, 1]
-
-    def rs_4(q):
-        i = mod4(pos[q][1] + 2)
+            for j in range(4):
+                add_to(q, t, o, h + j // 2, j % 2, r1[2 * q + t, k, j // 2, j % 2])
+            rs[q, t, 2, d] = push(gref(q, t, o, slice(None)), r2.at[2 * q + t, k], out_dev(q, d))
+
+    def rs_sum(q, t, di):
+        p, i = 2 * q + t, mod4(pos[q][1] + di)
+        for k in range(2):
+            add_to(q, t, pos[q][0], i, k, r2[p, 0, i, k], r2[p, 1, i, k])
+
+    def rs_3(q, t):
+        o, i = pos[q][0], mod4(pos[q][1] + 2)
+        for d in (1, -1):
+            rs[q, t, 2, d].wait_recv()
+        rs_sum(q, t, 2)
         for k, d in enumerate((1, -1)):
-            rs[q][4, d] = push(gpiece(q, i, k), r3.at[q, k], in_dev(q, d))
-
-    def rs_5(q):
+            rs[q, t, 4, d] = push(gref(q, t, o, i, k), r3.at[2 * q + t, k], in_dev(q, d))
+        for di in (1, -1, 0):
+            rs_sum(q, t, di)
+
+    def rs_5(q, t):
+        o = pos[q][0]
         for k, d in enumerate((1, -1)):
-            rs[q][4, d].wait_recv()
+            rs[q, t, 4, d].wait_recv()
             i = mod4(pos[q][1] + d)
-            add_to(q, pos[q][0], i, k, r3[q, k])
-            rs[q][5, d] = push(gpiece(q, i), r4.at[q, k], in_dev(q, d))
-
-    def rs_6(q):
-        for d in (1, -1):
-            rs[q][5, d].wait_recv()
-        for k in range(2):
-            add_to(q, pos[q][0], pos[q][1], k, r4[q, 0, k], r4[q, 1, k])
-        rs[q][6] = push(gpiece(q, pos[q][1], xl1), r5.at[q], xpair())
-
-    def rs_7(q):
-        rs[q][6].wait_recv()
-        total = g[gidx(q, pos[q][0], pos[q][1], xl)].astype(F32) + r5[q].astype(F32)
-        gin[:, q * 128 : (q + 1) * 128] = (total * shrink).T
+            add_to(q, t, o, i, k, r3[2 * q + t, k])
+            rs[q, t, 5, d] = push(gref(q, t, o, i), r4.at[2 * q + t, k], in_dev(q, d))
+
+    def rs_6(q, t):
+        o, i = pos[q]
+        for d in (1, -1):
+            rs[q, t, 5, d].wait_recv()
+        add_to(q, t, o, i, xl1, r4[2 * q + t, 0, xl1], r4[2 * q + t, 1, xl1])
+        rs[q, t, 6] = push(gref(q, t, o, i, xl1), r5.at[2 * q + t], xpair())
+        add_to(q, t, o, i, xl, r4[2 * q + t, 0, xl], r4[2 * q + t, 1, xl])
+
+    def rs_7(t):
+        for q in range(2):
+            rs[q, t, 6].wait_recv()
+            total = g[gat(q, t, *pos[q], xl)].astype(F32) + r5[2 * q + t].astype(F32)
+            gin_t[(2 * q + t) * 64 : (2 * q + t) * 64 + 64] = total * shrink
 
     def back():
         ld_up.wait()
@@ -315,8 +316,8 @@
             cols = pl.ds(pl.multiple_of(j * 1024, 1024), 1024)
             part = nn(bt[...], tok[:, cols]).astype(BF)
             for n in range(4):
-                for q in range(2):
-                    g[j // 2, (j % 2) * 2 + n // 2, n % 2, q] = part[q * 128 : q * 128 + 128, n * 256 : n * 256 + 256]
+                for p in range(4):
+                    g[j // 2, (j % 2) * 2 + n // 2, n % 2, p] = part[p * 64 : p * 64 + 64, n * 256 : n * 256 + 256]
             return carry
 
         lax.fori_loop(ks[0], ks[-1] + 1, one, 0)
@@ -369,7 +370,8 @@
         def one(k, carry):
             for cp in col_copies(k):
                 cp.wait()
-            part = nn(sl[k % 2], ag[k // 2, pl.ds((k % 2) * 2, 2)].reshape(1024, 256))
+            cy, cz = low_chunk(k)
+            part = nn(sl[k % 2], ag[cy, pl.ds(cz * 2, 2)].reshape(1024, 256))
             low[...] = jnp.where(k == 0, part, low[...] + part)
 
             @pl.when(k + 2 < 8)
@@ -464,17 +466,21 @@
 
     outs = []
 
-    def finish(ch):
+    def column_sums(ch):
         cols = slice(ch * 512, (ch + 1) * 512)
-        lowb = low[...].astype(BF)
         sums = jnp.zeros((1, 512), F32)
         for k in range(3):
             rows = slice(k * 256, (k + 1) * 256)
-            fo = acc[ch, rows]
-            mix = fo * scalev[:, cols] + ADAPTER_SCALE * nn(lowb[rows], upv[:, cols])
+            sums = sums + jnp.sum(cotv[rows, cols].astype(F32) * acc[ch, rows], axis=0, keepdims=True)
+        gs[0:1, cols] = sums * shrink
+
+    def mixture(ch):
+        cols = slice(ch * 512, (ch + 1) * 512)
+        lowb = low[...].astype(BF)
+        for k in range(3):
+            rows = slice(k * 256, (k + 1) * 256)
+            mix = acc[ch, rows] * scalev[:, cols] + ADAPTER_SCALE * nn(lowb[rows], upv[:, cols])
             val[rows, cols] = mix.astype(BF)
-            sums = sums + jnp.sum(cotv[rows, cols].astype(F32) * fo, axis=0, keepdims=True)
-        gs[0:1, cols] = sums * shrink
 
     sx = {}
 
@@ -500,9 +506,13 @@
         gs[3:4] = (gs[2:3] + gs_o[5:6]) + (gs_o[3:4] + gs_o[4:5])
         return [local(gs.at[3:4], o_gs)]
 
-    def both(fn):
-        fn(0)
-        fn(1)
+    def both(fn, *args):
+        fn(0, *args)
+        fn(1, *args)
+
+    def drain(keep):
+        while len(sent) > keep:
+            sent.pop(0).wait_send()
 
     def use(far, do):
         for q in range(2):
@@ -530,46 +540,57 @@
     outs += frag_1()
     use(0, 0)
     both(w_6)
-    both(rs_1)
     use(0, 1)
     use(0, -1)
+    frag_2()
+    both(a_out2)
+    both(rs_1, 0)
+    both(rs_1, 1)
+    low_rank(0, 3)
     for q in range(2):
         w_7(q, 0)
-    frag_2()
     use(0, 2)
-    both(a_out2)
     use(1, 0)
-    both(rs_2)
     for do in (1, -1):
         for q in range(2):
             w_7(q, do)
     both(a_out3)
-    low_rank(0, 8)
+    both(rs_2, 0)
+    both(rs_2, 1)
+    low_rank(3, 8)
     gout_1()
-    both(rs_3)
-    both(rs_4)
     use(1, 1)
     use(1, -1)
+    for q in range(2):
+        w_7(q, 2)
     frag_3()
+    use(1, 2)
+    for ch in range(2):
+        column_sums(ch)
+    scale_x()
+    both(rs_3, 0)
+    both(rs_3, 1)
+    ld_sc.wait()
+    mixture(0)
     gout_2()
     gout_2s()
-    both(rs_5)
-    for q in range(2):
-        w_7(q, 2)
-    both(rs_6)
+    both(rs_5, 0)
+    both(rs_5, 1)
+    scale_i()
+    mixture(1)
+    outs.append(local(val, o_val))
     outs += frag_4()
-    use(1, 2)
-    ld_sc.wait()
-    for ch in range(2):
-        finish(ch)
-    scale_x()
-    outs.append(local(val, o_val))
+    drain(24)
     gout_3()
-    scale_i()
-    both(rs_7)
-    outs.append(local(gin, o_gin))
+    both(rs_6, 0)
+    both(rs_6, 1)
     scale_o()
     outs += gout_4()
+    drain(7)
+    rs_7(0)
+    rs_7(1)
+    gin[...] = gin_t[...].T
+    outs.append(local(gin, o_gin))
     outs += scale_f()
     for cp in sent:
         cp.wait_send()
@@ -598,12 +619,12 @@
         vm((16, 8192), BF),
         vm((16, 8192), BF),
         vm((2, ROWS, 1024), BF),
-        vm((4, 4, 2, 2, 128, 256), BF),
-        vm((2, 2, 2, 2, 128, 256), BF),
-        vm((2, 2, 4, 2, 128, 256), BF),
-        vm((2, 2, 128, 256), BF),
-        vm((2, 2, 2, 128, 256), BF),
-        vm((2, 128, 256), BF),
+        vm((4, 4, 2, 4, 64, 256), BF),
+        vm((4, 2, 2, 2, 64, 256), BF),
+        vm((4, 2, 4, 2, 64, 256), BF),
+        vm((4, 2, 64, 256), BF),
+        vm((4, 2, 2, 64, 256), BF),
+        vm((4, 64, 256), BF),
         vm((ROWS, 1024), BF),
         vm((256, 1024), BF),
         vm((2, ROWS, 512), F32),
@@ -629,6 +650,7 @@
         vm((512, 256), BF),
         vm((16, 1024), BF),
         vm((256, 256), F32),
+        vm((256, 256), F32),
         vm((2, 8, 1024), F32),
         pltpu.SemaphoreType.DMA((NSEM,)),
         pltpu.SemaphoreType.DMA((NSEM,)),
@@ -652,12 +674,17 @@
 
 def hand_over(refs):
     n = len(refs)
+    parts = []
+    for k, a in enumerate(refs):
+        parts.append((k, pl.ds(0, a.shape[0])))
 
     def copy_all(*args):
         src, dst, held = args[:n], args[n : 2 * n], args[2 * n : 3 * n]
         sem_in, sem_out = args[3 * n :]
-        into = [pltpu.make_async_copy(a, b, sem_in.at[k]) for k, (a, b) in enumerate(zip(src, held))]
-        away = [pltpu.make_async_copy(a, b, sem_out.at[k]) for k, (a, b) in enumerate(zip(held, dst))]
+        into, away = [], []
+        for m, (k, rows) in enumerate(parts):
+            into.append(pltpu.make_async_copy(src[k].at[rows], held[k].at[rows], sem_in.at[m]))
+            away.append(pltpu.make_async_copy(held[k].at[rows], dst[k].at[rows], sem_out.at[m]))
         for cp in into:
             cp.start()
         for a, b in zip(into, away):
@@ -674,7 +701,7 @@
         in_specs=[hbm] * n,
         out_specs=[hbm] * n,
         scratch_shapes=[pltpu.VMEM(a.shape, a.dtype) for a in refs]
-        + [pltpu.SemaphoreType.DMA((n,)), pltpu.SemaphoreType.DMA((n,))],
+        + [pltpu.SemaphoreType.DMA((len(parts),))] * 2,
         compiler_params=pltpu.CompilerParams(vmem_limit_bytes=60 * 1024 * 1024),
     )(*refs)
 

time: 104 us -> 96.7 us (0.930)
  Pallas kernels: 102 us -> 94.5 us
    pallas_call x1, Pallas kernels: 98.2 us -> 90.5 us  [call(): pl.pallas_call(body, name='step', out_shape=out, in_specs=[hbm] * len(arg...]
where the time goes in v3:
time: 96.7 us; the launch traced here: 95.4 us
  Pallas kernels  94.5 us (98%)
    pallas_call x1, Pallas kernels, call(): pl.pallas_call(body, name='step', out_shape=out, in_specs=[hbm] * len(arg...  90.5 us
    pallas_call x1, Pallas kernels, hand_over(): pl.pallas_call(copy_all, name='hand_over', out_shape=[jax.ShapeDtypeStruc...  4.09 us

profile of v3, /device:TPU:0, one launch (start us, length us, event | category | flops | bytes accessed | tf_op | source)
XLA Modules:
  0.0 95.4 jit_solution(4411998299940767188)
XLA Ops:
  0.6 90.5 %step.1 = (bf16[768,1024]{1,0:T(8,128)(2,1)}, f32[256,256]{1,0:T(8,128)}, f32[8,1024]{1,0:T(8,128)}, f32[1,1024]{1,0:T(1,128)}, f32[1024,256]{1,0:T(8,128)}, /*i...) custom-call(bf16[768,8192]{1,0:T(8,128)(2,1)} %tokens.1, ...), custom_call_target="tpu_custom_call" | custom-call | flops 23000000512 | bytes 30000000 | tf_op jit(solution)/shard_map/step/pallas_call | solution.py:661
  91.1 4.1 %hand_over.1 = (bf16[768,1024]{1,0:T(8,128)(2,1)}, f32[1,256,256]{2,1,0:T(8,128)}, f32[1,8,1024]{2,1,0:T(8,128)}, f32[1,1024]{1,0:T(1,128)}, f32[4,256,256]{2,1,...) custom-call(bf16[768,1024]{1,0:T(8,128)(2,1)} %get-tuple-element.20., ...), custom_call_target="tpu_custom_call" | custom-call | tf_op jit(solution)/shard_map/hand_over/pallas_call | solution.py:697

commit v4 on v3

--- a/solution.py
+++ b/solution.py
@@ -277,6 +277,8 @@
         rs_sum(q, t, 2)
         for k, d in enumerate((1, -1)):
             rs[q, t, 4, d] = push(gref(q, t, o, i, k), r3.at[2 * q + t, k], in_dev(q, d))
+
+    def rs_4(q, t):
         for di in (1, -1, 0):
             rs_sum(q, t, di)
 
@@ -542,7 +544,6 @@
     both(w_6)
     use(0, 1)
     use(0, -1)
-    frag_2()
     both(a_out2)
     both(rs_1, 0)
     both(rs_1, 1)
@@ -554,44 +555,46 @@
     for do in (1, -1):
         for q in range(2):
             w_7(q, do)
+    use(1, 1)
     both(a_out3)
     both(rs_2, 0)
     both(rs_2, 1)
+    use(1, -1)
     low_rank(3, 8)
     gout_1()
-    use(1, 1)
-    use(1, -1)
     for q in range(2):
         w_7(q, 2)
-    frag_3()
+    frag_2()
     use(1, 2)
     for ch in range(2):
         column_sums(ch)
     scale_x()
+    ld_sc.wait()
+    mixture(0)
     both(rs_3, 0)
     both(rs_3, 1)
-    ld_sc.wait()
-    mixture(0)
+    scale_i()
+    both(rs_4, 0)
+    both(rs_4, 1)
     gout_2()
     gout_2s()
+    frag_3()
     both(rs_5, 0)
     both(rs_5, 1)
-    scale_i()
     mixture(1)
     outs.append(local(val, o_val))
-    outs += frag_4()
-    drain(24)
-    gout_3()
+    scale_o()
     both(rs_6, 0)
     both(rs_6, 1)
-    scale_o()
-    outs += gout_4()
-    drain(7)
+    gout_3()
+    drain(24)
+    outs += scale_f()
+    outs += frag_4()
     rs_7(0)
     rs_7(1)
     gin[...] = gin_t[...].T
     outs.append(local(gin, o_gin))
-    outs += scale_f()
+    outs += gout_4()
     for cp in sent:
         cp.wait_send()
     for cp in outs:

time: 96.7 us -> 96.3 us (level)
  no operation moved by 1% of the time
where the time goes in v4:
time: 96.3 us; the launch traced here: 95.4 us
  Pallas kernels  94.6 us (98%)
    pallas_call x1, Pallas kernels, call(): pl.pallas_call(body, name='step', out_shape=out, in_specs=[hbm] * len(arg...  90.5 us
    pallas_call x1, Pallas kernels, hand_over(): pl.pallas_call(copy_all, name='hand_over', out_shape=[jax.ShapeDtypeStruc...  4.09 us

profile of v4, /device:TPU:0, one launch (start us, length us, event | category | flops | bytes accessed | tf_op | source)
XLA Modules:
  0.0 95.4 jit_solution(4585003812796957766)
XLA Ops:
  0.6 90.5 %step.1 = (bf16[768,1024]{1,0:T(8,128)(2,1)}, f32[256,256]{1,0:T(8,128)}, f32[8,1024]{1,0:T(8,128)}, f32[1,1024]{1,0:T(1,128)}, f32[1024,256]{1,0:T(8,128)}, /*i...) custom-call(bf16[768,8192]{1,0:T(8,128)(2,1)} %tokens.1, ...), custom_call_target="tpu_custom_call" | custom-call | flops 23000000512 | bytes 30000000 | tf_op jit(solution)/shard_map/step/pallas_call | solution.py:664
  91.1 4.1 %hand_over.1 = (bf16[768,1024]{1,0:T(8,128)(2,1)}, f32[1,256,256]{2,1,0:T(8,128)}, f32[1,8,1024]{2,1,0:T(8,128)}, f32[1,1024]{1,0:T(1,128)}, f32[4,256,256]{2,1,...) custom-call(bf16[768,1024]{1,0:T(8,128)(2,1)} %get-tuple-element.20., ...), custom_call_target="tpu_custom_call" | custom-call | tf_op jit(solution)/shard_map/hand_over/pallas_call | solution.py:700
